TPU v7x, 32 devices: a whole 2x2x4 slice. The times are simulated.
32 devices in a mesh: gy: 8 (over y, x, core), gx: 4 (over z).
Axes of the slice: x: 2, y: 2, z: 4, core: 2. Of those that a mesh axis runs over, the one named last changes fastest.
Arguments:
- features: bfloat16 [256, 256, 128], P('gy', 'gx'), may hold values from -6 to 6
- station_mask: int32 [256, 256], P('gy', 'gx'), may hold values 0 or 1
- station_gain: float32 [128], replicated, may hold values from -4 to 4
- fine_kernel: bfloat16 [3, 3, 128, 128], replicated, may hold values from -0.1875 to 0.1875
- down_mid: bfloat16 [128, 256], replicated, may hold values from -0.5 to 0.5
- mid_kernel: bfloat16 [3, 3, 256, 256], replicated, may hold values from -0.125 to 0.125
- down_coarse: bfloat16 [256, 512], replicated, may hold values from -0.375 to 0.375
- coarse_kernel: bfloat16 [3, 3, 512, 512], P(None, None, None, 'gx'), may hold values from -0.09375 to 0.09375
- up_coarse: bfloat16 [512, 256], replicated, may hold values from -0.25 to 0.25
- central_lifted_mixing: bfloat16 [256, 128], replicated, may hold values from -0.375 to 0.375
- cotangent: bfloat16 [256, 256, 128], P('gy', 'gx'), may hold values from -6 to 6
Outputs:
- predicted_rainfall: bfloat16 [256, 256, 128], P('gy', 'gx')
- hidden_maps_sensitivity: bfloat16 [256, 256, 128], P('gy', 'gx')
- sharpest_filter_derivative: float32 [3, 3, 128, 128], replicated
All inputs are finite; a program needn't handle non-finite values. No bound on the sum of `station_mask` on one device may be relied on, other than what follows from the above.
Results may differ from a plain program's by a relative error of at most 0.0095.
Values may be sent and summed in bfloat16 or wider, within the bound.
A program may use at most 64 MiB of HBM per device.

v0:
```python
import jax
import jax.numpy as jnp
from jax import lax
from jax.sharding import PartitionSpec as P


def with_halo(x, sides, width):
    for axis, dim in sides:
        size, length = (lax.axis_size(axis), x.shape[dim])
        up = [(i, (i + 1) % size) for i in range(size - 1)]
        down = [(j, i) for i, j in up]
        last = lax.slice_in_dim(x, length - width, length, axis=dim)
        leading = lax.slice_in_dim(x, 0, width, axis=dim)
        before = lax.ppermute(last, axis, up)
        after = lax.ppermute(leading, axis, down)
        x = jnp.concatenate([before, x, after], axis=dim)
    return x


def conv_valid(padded, kernel):
    rows = padded.shape[0] - 2
    cols = padded.shape[1] - 2
    total = jnp.zeros((rows * cols, kernel.shape[3]), jnp.float32)
    for row_off in range(3):
        for col_off in range(3):
            window = padded[row_off : row_off + rows, col_off : col_off + cols].reshape(
                rows * cols, -1
            )
            total = total + jnp.dot(
                window, kernel[row_off, col_off], preferred_element_type=jnp.float32
            )
    return total.reshape(rows, cols, kernel.shape[3])


def convt_valid(padded, kernel):
    rows = padded.shape[0] - 2
    cols = padded.shape[1] - 2
    total = jnp.zeros((rows * cols, kernel.shape[2]), jnp.float32)
    for row_off in range(3):
        for col_off in range(3):
            window = padded[
                2 - row_off : 2 - row_off + rows, 2 - col_off : 2 - col_off + cols
            ].reshape(rows * cols, -1)
            total = total + lax.dot_general(
                window,
                kernel[row_off, col_off],
                (((1,), (1,)), ((), ())),
                preferred_element_type=jnp.float32,
            )
    return total.reshape(rows, cols, kernel.shape[2])


def kernel_grad(padded, delta):
    rows = padded.shape[0] - 2
    cols = padded.shape[1] - 2
    flat_delta = delta.reshape(rows * cols, -1)
    blocks = []
    for row_off in range(3):
        line = []
        for col_off in range(3):
            window = padded[row_off : row_off + rows, col_off : col_off + cols].reshape(
                rows * cols, -1
            )
            line.append(
                lax.dot_general(
                    window, flat_delta, (((0,), (0,)), ((), ())), preferred_element_type=jnp.float32
                )
            )
        blocks.append(jnp.stack(line))
    return jnp.stack(blocks)


def pool_mean(field):
    rows, cols, chans = field.shape
    return (
        field.astype(jnp.float32)
        .reshape(rows // 2, 2, cols // 2, 2, chans)
        .mean(axis=(1, 3))
        .astype(jnp.bfloat16)
    )


def block_sum(field):
    rows, cols, chans = field.shape
    return field.astype(jnp.float32).reshape(rows // 2, 2, cols // 2, 2, chans).sum(axis=(1, 3))


def double_spatial_lattice(field):
    return jnp.repeat(jnp.repeat(field, 2, axis=0), 2, axis=1)


def pointwise_mixing_weights(field, matrix):
    rows, cols, chans = field.shape
    return jnp.dot(
        field.reshape(rows * cols, chans), matrix, preferred_element_type=jnp.float32
    ).reshape(rows, cols, -1)


def project_back(field, matrix):
    rows, cols, chans = field.shape
    out = lax.dot_general(
        field.reshape(rows * cols, chans),
        matrix,
        (((1,), (1,)), ((), ())),
        preferred_element_type=jnp.float32,
    )
    return out.reshape(rows, cols, -1)


def silu_slope(value):
    sig = jax.nn.sigmoid(value)
    return sig * (1.0 + value * (1.0 - sig))


def rims_fine(field):
    return with_halo(field, (("gy", 0), ("gx", 1)), 1)


def rims_mid(field):
    return with_halo(field, (("gy", 0), ("gx", 1)), 1)


def rims_coarse(field):
    return with_halo(field, (("gy", 0), ("gx", 1)), 1)


def shards(
    features,
    station_mask,
    station_gain,
    fine_kernel,
    down_mid,
    mid_kernel,
    down_coarse,
    coarse_kernel,
    up_coarse,
    central_lifted_mixing,
    cotangent,
):
    inputs = (
        features.astype(jnp.float32)
        + station_mask.astype(jnp.float32)[:, :, None] * station_gain[None, None, :]
    ).astype(jnp.bfloat16)
    in_pad = rims_fine(inputs)
    pre_fine = conv_valid(in_pad, fine_kernel)
    sharpest_level_response = jax.nn.silu(pre_fine).astype(jnp.bfloat16)
    mid_in = pointwise_mixing_weights(pool_mean(sharpest_level_response), down_mid).astype(
        jnp.bfloat16
    )
    pre_mid = conv_valid(rims_mid(mid_in), mid_kernel)
    act_mid = jax.nn.silu(pre_mid).astype(jnp.bfloat16)
    coarse_in = pointwise_mixing_weights(pool_mean(act_mid), down_coarse).astype(jnp.bfloat16)
    coarse_pad = rims_coarse(coarse_in)
    pre_coarse = conv_valid(coarse_pad, lax.all_gather(coarse_kernel, "gx", axis=3, tiled=True))
    act_coarse = jax.nn.silu(pre_coarse).astype(jnp.bfloat16)
    ascend_central_level = (
        double_spatial_lattice(pointwise_mixing_weights(act_coarse, up_coarse))
        + act_mid.astype(jnp.float32)
    ).astype(jnp.bfloat16)
    predicted_rainfall = (
        double_spatial_lattice(
            pointwise_mixing_weights(ascend_central_level, central_lifted_mixing)
        )
        + sharpest_level_response.astype(jnp.float32)
    ).astype(jnp.bfloat16)
    back_mid = block_sum(cotangent).astype(jnp.bfloat16)
    grad_mid = project_back(back_mid, central_lifted_mixing)
    back_coarse = block_sum(grad_mid).astype(jnp.bfloat16)
    delta_coarse = (project_back(back_coarse, up_coarse) * silu_slope(pre_coarse)).astype(
        jnp.bfloat16
    )
    delta_pad = rims_coarse(delta_coarse)
    into_total = convt_valid(delta_pad, lax.all_gather(coarse_kernel, "gx", axis=3, tiled=True))
    into_coarse = into_total.astype(jnp.bfloat16)
    delta_mid = (
        (grad_mid + double_spatial_lattice(project_back(into_coarse, down_coarse)) * 0.25)
        * silu_slope(pre_mid)
    ).astype(jnp.bfloat16)
    into_mid = convt_valid(rims_mid(delta_mid), mid_kernel).astype(jnp.bfloat16)
    delta_fine = (
        (
            cotangent.astype(jnp.float32)
            + double_spatial_lattice(project_back(into_mid, down_mid)) * 0.25
        )
        * silu_slope(pre_fine)
    ).astype(jnp.bfloat16)
    local_grad = kernel_grad(in_pad, delta_fine)
    cells_all = features.shape[0] * lax.axis_size("gy") * features.shape[1] * lax.axis_size("gx")
    scale = 1.0 / jnp.sqrt(jnp.float32(cells_all))
    sharpest_filter_derivative = lax.psum(local_grad, ("gy", "gx")) * scale
    hidden_maps_sensitivity = convt_valid(rims_fine(delta_fine), fine_kernel).astype(jnp.bfloat16)
    return (predicted_rainfall, hidden_maps_sensitivity, sharpest_filter_derivative)


def solution(mesh):
    return jax.shard_map(
        shards,
        mesh=mesh,
        in_specs=(
            P("gy", "gx", None),
            P("gy", "gx"),
            P(),
            P(),
            P(),
            P(),
            P(),
            P(None, None, None, "gx"),
            P(),
            P(),
            P("gy", "gx", None),
        ),
        out_specs=(P("gy", "gx", None), P("gy", "gx", None), P()),
        check_vma=False,
    )
```

profile of v0, /device:TPU:0, one launch (start us, length us, event | category | flops | bytes accessed | tf_op | source)
XLA Modules:
  0.0 322.3 jit_solution(14048423227385101666)
XLA Ops:
  8.0 1.4 add_convert_fusion.1
  10.7 3.0 collective-permute-start
  14.6 4.9 %collective-permute-start.2 = (bf16[34,1,128]{2,1,0:T(2,128)(2,1)S(1)}, bf16[34,1,128]{2,1,0:T(2,128)(2,1)S(1)}, u32[]{:S(2)}, u32[]{:S(2)}) collective-permute-start(bf16[34,1,128]{2,1,0:T(2,128)(2,1)S(1)} %get-tuple-element.23), channel_id=1, source_target_pairs={{0,1},{1,2},{2,3},{4,5},{5,6},{6,7},{8,9},{9,10},{10,11},{12,13},{... | collective-permute-start | bytes 26120 | tf_op jit(solution)/shard_map/ppermute | solution.py:14
  21.2 4.0 %collective-permute-done.3 = bf16[34,1,128]{2,1,0:T(2,128)(2,1)S(1)} collective-permute-done((bf16[34,1,128]{2,1,0:T(2,128)(2,1)S(1)}, bf16[34,1,128]{2,1,0:T(2,128)(2,1)S(1)}, u32[]{:S(2)}, u32[]{:S(2)}) %collective-permute-start.3) | collective-permute-done | bytes 8736 | tf_op jit(solution)/shard_map/ppermute | solution.py:15
  31.1 3.0 collective-permute-start.4
  34.1 1.6 reduce_sum.38
  35.8 3.5 %collective-permute-start.6 = (bf16[18,1,256]{2,1,0:T(2,128)(2,1)S(1)}, bf16[18,1,256]{2,1,0:T(2,128)(2,1)S(1)}, u32[]{:S(2)}, u32[]{:S(2)}) collective-permute-start(bf16[18,1,256]{2,1,0:T(2,128)(2,1)S(1)} %get-tuple-element.51), channel_id=1, source_target_pairs={{0,1},{1,2},{2,3},{4,5},{5,6},{6,7},{8,9},{9,10},{10,11},{12,13},{... | collective-permute-start | bytes 27656 | tf_op jit(solution)/shard_map/ppermute | solution.py:14
  42.6 13.5 %collective-permute-done.7 = bf16[18,1,256]{2,1,0:T(2,128)(2,1)S(1)} collective-permute-done((bf16[18,1,256]{2,1,0:T(2,128)(2,1)S(1)}, bf16[18,1,256]{2,1,0:T(2,128)(2,1)S(1)}, u32[]{:S(2)}, u32[]{:S(2)}) %collective-permute-start.7) | collective-permute-done | bytes 9248 | tf_op jit(solution)/shard_map/ppermute | solution.py:15
  58.8 1.8 convolution_convert_fusion.1
  63.3 3.6 %collective-permute-start.8 = (bf16[1,16,512]{2,1,0:T(8,128)(2,1)}, bf16[1,16,512]{2,1,0:T(8,128)(2,1)}, u32[]{:S(2)}, u32[]{:S(2)}) collective-permute-start(bf16[1,16,512]{2,1,0:T(8,128)(2,1)} %get-tuple-element.87), channel_id=1, source_target_pairs={{0,4},{4,8},{8,12},{12,16},{16,20},{20,24},{24,28},{1,5},{5,9},{9,... | collective-permute-start | bytes 49160 | tf_op jit(solution)/shard_map/ppermute | solution.py:14
  68.2 2.0 reduce_sum.39
  73.8 1.7 pad_maximum_fusion.17
  75.6 4.8 %collective-permute-done.11 = bf16[10,1,512]{2,1,0:T(2,128)(2,1)S(1)} collective-permute-done((bf16[10,1,512]{2,1,0:T(2,128)(2,1)S(1)}, bf16[10,1,512]{2,1,0:T(2,128)(2,1)S(1)}, u32[]{:S(2)}, u32[]{:S(2)}) %collective-permute-start.11) | collective-permute-done | bytes 10272 | tf_op jit(solution)/shard_map/ppermute | solution.py:15
  82.9 24.3 %all-gather.2.cloned.1.call-done = bf16[3,3,512,512]{3,2,1,0:T(8,128)(2,1)} async-done(((bf16[3,3,512,128]{3,2,1,0:T(8,128)(2,1)}), bf16[3,3,512,512]{3,2,1,0:T(8,128)(2,1)}) %all-gather.2.cloned.1.call-update) | async-done | bytes 4718608 | tf_op jit(solution)/shard_map/all_gather | solution.py:154
  107.2 1.4 fusion.19
  113.8 1.3 convolution_add_fusion.38
  117.8 1.4 multiply_convert_fusion.8
  122.0 3.6 %collective-permute-start.12 = (bf16[1,16,512]{2,1,0:T(8,128)(2,1)}, bf16[1,16,512]{2,1,0:T(8,128)(2,1)}, u32[]{:S(2)}, u32[]{:S(2)}) collective-permute-start(bf16[1,16,512]{2,1,0:T(8,128)(2,1)} %get-tuple-element.83), channel_id=1, source_target_pairs={{0,4},{4,8},{8,12},{12,16},{16,20},{20,24},{24,28},{1,5},{5,9},{9,... | collective-permute-start | bytes 49160 | tf_op jit(solution)/shard_map/ppermute | solution.py:14
  126.8 2.2 reshape.292
  129.0 2.1 add_convert_fusion.2
  133.2 4.7 %collective-permute-start.15 = (bf16[10,1,512]{2,1,0:T(2,128)(2,1)S(1)}, bf16[10,1,512]{2,1,0:T(2,128)(2,1)S(1)}, u32[]{:S(2)}, u32[]{:S(2)}) collective-permute-start(bf16[10,1,512]{2,1,0:T(2,128)(2,1)S(1)} %get-tuple-element.76), channel_id=1, source_target_pairs={{0,1},{1,2},{2,3},{4,5},{5,6},{6,7},{8,9},{9,10},{10,11},{12,13},{... | collective-permute-start | bytes 30728 | tf_op jit(solution)/shard_map/ppermute | solution.py:14
  142.4 1.3 convolution_add_fusion.34
  143.7 1.3 convolution_add_fusion.33
  148.3 2.2 mul.119
  153.7 3.6 %collective-permute-start.16 = (bf16[1,32,256]{2,1,0:T(8,128)(2,1)}, bf16[1,32,256]{2,1,0:T(8,128)(2,1)}, u32[]{:S(2)}, u32[]{:S(2)}) collective-permute-start(bf16[1,32,256]{2,1,0:T(8,128)(2,1)} %get-tuple-element.55), channel_id=1, source_target_pairs={{0,4},{4,8},{8,12},{12,16},{16,20},{20,24},{24,28},{1,5},{5,9},{9,... | collective-permute-start | bytes 49160 | tf_op jit(solution)/shard_map/ppermute | solution.py:14
  158.2 2.2 mul.123
  162.5 4.5 %collective-permute-start.19 = (bf16[18,1,256]{2,1,0:T(2,128)(2,1)S(1)}, bf16[18,1,256]{2,1,0:T(2,128)(2,1)S(1)}, u32[]{:S(2)}, u32[]{:S(2)}) collective-permute-start(bf16[18,1,256]{2,1,0:T(2,128)(2,1)S(1)} %get-tuple-element.48), channel_id=1, source_target_pairs={{0,1},{1,2},{2,3},{4,5},{5,6},{6,7},{8,9},{9,10},{10,11},{12,13},{... | collective-permute-start | bytes 27656 | tf_op jit(solution)/shard_map/ppermute | solution.py:14
  175.2 1.4 multiply_convert_fusion
  180.3 3.0 collective-permute-start.20
  186.3 4.8 %collective-permute-start.23 = (bf16[34,1,128]{2,1,0:T(2,128)(2,1)S(1)}, bf16[34,1,128]{2,1,0:T(2,128)(2,1)S(1)}, u32[]{:S(2)}, u32[]{:S(2)}) collective-permute-start(bf16[34,1,128]{2,1,0:T(2,128)(2,1)S(1)} %get-tuple-element.20), channel_id=1, source_target_pairs={{0,1},{1,2},{2,3},{4,5},{5,6},{6,7},{8,9},{9,10},{10,11},{12,13},{... | collective-permute-start | bytes 26120 | tf_op jit(solution)/shard_map/ppermute | solution.py:14
  196.7 116.8 %all-reduce.2.cloned.1.call-done = f32[3,3,128,128]{3,2,1,0:T(8,128)} async-done(((f32[3,3,128,128]{3,2,1,0:T(8,128)}), f32[3,3,128,128]{3,2,1,0:T(8,128)}) %all-reduce.2.cloned.1.call-update) | async-done | bytes 589840 | tf_op jit(solution)/shard_map/psum | solution.py:190
  313.6 1.9 broadcast_multiply_fusion
  (224 shorter events, 73.9 us)
Async XLA Ops:
  7.2 112.0 %copy-start = (bf16[512,256]{1,0:T(8,128)(2,1)S(1)}, bf16[512,256]{1,0:T(8,128)(2,1)}, u32[]{:S(2)}) copy-start(bf16[512,256]{1,0:T(8,128)(2,1)} %param.19) | copy-start | bytes 786436
  7.2 100.0 %all-gather.2.cloned.1.call-start = ((), (), s32[]{:S(2)}) async-start(), calls=%async_computation | async-start | bytes 5898240 | tf_op jit(solution)/shard_map/all_gather | solution.py:154
  9.4 4.4 %collective-permute-start.1 = (bf16[1,64,128]{2,1,0:T(8,128)(2,1)S(1)}, bf16[1,64,128]{2,1,0:T(8,128)(2,1)S(1)}, u32[]{:S(2)}, u32[]{:S(2)}) collective-permute-start(bf16[1,64,128]{2,1,0:T(8,128)(2,1)S(1)} %get-tuple-element.32), channel_id=1, source_target_pairs={{4,0},{8,4},{12,8},{16,12},{20,16},{24,20},{28,24},{5,1},{9,5},{13... | collective-permute-start | bytes 49160 | tf_op jit(solution)/shard_map/ppermute | solution.py:15
  10.7 3.9 %collective-permute-start = (bf16[1,64,128]{2,1,0:T(8,128)(2,1)S(1)}, bf16[1,64,128]{2,1,0:T(8,128)(2,1)S(1)}, u32[]{:S(2)}, u32[]{:S(2)}) collective-permute-start(bf16[1,64,128]{2,1,0:T(8,128)(2,1)S(1)} %get-tuple-element.31), channel_id=1, source_target_pairs={{0,4},{4,8},{8,12},{12,16},{16,20},{20,24},{24,28},{1,5},{5,9},{9,... | collective-permute-start | bytes 49160 | tf_op jit(solution)/shard_map/ppermute | solution.py:14
  13.8 299.8 %all-reduce.2.cloned.1.call-start = ((), (), s32[]{:S(2)}) async-start(), calls=%async_computation.1 | async-start | bytes 1179648 | tf_op jit(solution)/shard_map/psum | solution.py:190
  14.6 6.6 %collective-permute-start.2 = (bf16[34,1,128]{2,1,0:T(2,128)(2,1)S(1)}, bf16[34,1,128]{2,1,0:T(2,128)(2,1)S(1)}, u32[]{:S(2)}, u32[]{:S(2)}) collective-permute-start(bf16[34,1,128]{2,1,0:T(2,128)(2,1)S(1)} %get-tuple-element.23), channel_id=1, source_target_pairs={{0,1},{1,2},{2,3},{4,5},{5,6},{6,7},{8,9},{9,10},{10,11},{12,13},{... | collective-permute-start | bytes 26120 | tf_op jit(solution)/shard_map/ppermute | solution.py:14
  19.5 5.7 %collective-permute-start.3 = (bf16[34,1,128]{2,1,0:T(2,128)(2,1)S(1)}, bf16[34,1,128]{2,1,0:T(2,128)(2,1)S(1)}, u32[]{:S(2)}, u32[]{:S(2)}) collective-permute-start(bf16[34,1,128]{2,1,0:T(2,128)(2,1)S(1)} %get-tuple-element.24), channel_id=1, source_target_pairs={{1,0},{2,1},{3,2},{5,4},{6,5},{7,6},{9,8},{10,9},{11,10},{13,12},{... | collective-permute-start | bytes 26120 | tf_op jit(solution)/shard_map/ppermute | solution.py:15
  29.8 6.0 %collective-permute-start.5 = (bf16[1,32,256]{2,1,0:T(8,128)(2,1)S(1)}, bf16[1,32,256]{2,1,0:T(8,128)(2,1)S(1)}, u32[]{:S(2)}, u32[]{:S(2)}) collective-permute-start(bf16[1,32,256]{2,1,0:T(8,128)(2,1)S(1)} %get-tuple-element.60), channel_id=1, source_target_pairs={{4,0},{8,4},{12,8},{16,12},{20,16},{24,20},{28,24},{5,1},{9,5},{13... | collective-permute-start | bytes 49160 | tf_op jit(solution)/shard_map/ppermute | solution.py:15
  31.1 4.7 %collective-permute-start.4 = (bf16[1,32,256]{2,1,0:T(8,128)(2,1)S(1)}, bf16[1,32,256]{2,1,0:T(8,128)(2,1)S(1)}, u32[]{:S(2)}, u32[]{:S(2)}) collective-permute-start(bf16[1,32,256]{2,1,0:T(8,128)(2,1)S(1)} %get-tuple-element.59), channel_id=1, source_target_pairs={{0,4},{4,8},{8,12},{12,16},{16,20},{20,24},{24,28},{1,5},{5,9},{9,... | collective-permute-start | bytes 49160 | tf_op jit(solution)/shard_map/ppermute | solution.py:14
  35.8 6.8 %collective-permute-start.6 = (bf16[18,1,256]{2,1,0:T(2,128)(2,1)S(1)}, bf16[18,1,256]{2,1,0:T(2,128)(2,1)S(1)}, u32[]{:S(2)}, u32[]{:S(2)}) collective-permute-start(bf16[18,1,256]{2,1,0:T(2,128)(2,1)S(1)} %get-tuple-element.51), channel_id=1, source_target_pairs={{0,1},{1,2},{2,3},{4,5},{5,6},{6,7},{8,9},{9,10},{10,11},{12,13},{... | collective-permute-start | bytes 27656 | tf_op jit(solution)/shard_map/ppermute | solution.py:14
  39.3 16.8 %collective-permute-start.7 = (bf16[18,1,256]{2,1,0:T(2,128)(2,1)S(1)}, bf16[18,1,256]{2,1,0:T(2,128)(2,1)S(1)}, u32[]{:S(2)}, u32[]{:S(2)}) collective-permute-start(bf16[18,1,256]{2,1,0:T(2,128)(2,1)S(1)} %get-tuple-element.52), channel_id=1, source_target_pairs={{1,0},{2,1},{3,2},{5,4},{6,5},{7,6},{9,8},{10,9},{11,10},{13,12},{... | collective-permute-start | bytes 27656 | tf_op jit(solution)/shard_map/ppermute | solution.py:15
  40.6 15.5 %copy-start.27 = (bf16[1,32,256]{2,1,0:T(8,128)(2,1)S(1)}, bf16[1,32,256]{2,1,0:T(8,128)(2,1)}, u32[]{:S(2)}) copy-start(bf16[1,32,256]{2,1,0:T(8,128)(2,1)} %copy-done.26) | copy-start | bytes 49156
  62.0 8.3 %collective-permute-start.9 = (bf16[1,16,512]{2,1,0:T(8,128)(2,1)}, bf16[1,16,512]{2,1,0:T(8,128)(2,1)}, u32[]{:S(2)}, u32[]{:S(2)}) collective-permute-start(bf16[1,16,512]{2,1,0:T(8,128)(2,1)} %get-tuple-element.88), channel_id=1, source_target_pairs={{4,0},{8,4},{12,8},{16,12},{20,16},{24,20},{28,24},{5,1},{9,5},{13... | collective-permute-start | bytes 49160 | tf_op jit(solution)/shard_map/ppermute | solution.py:15
  63.3 7.0 %collective-permute-start.8 = (bf16[1,16,512]{2,1,0:T(8,128)(2,1)}, bf16[1,16,512]{2,1,0:T(8,128)(2,1)}, u32[]{:S(2)}, u32[]{:S(2)}) collective-permute-start(bf16[1,16,512]{2,1,0:T(8,128)(2,1)} %get-tuple-element.87), channel_id=1, source_target_pairs={{0,4},{4,8},{8,12},{12,16},{16,20},{20,24},{24,28},{1,5},{5,9},{9,... | collective-permute-start | bytes 49160 | tf_op jit(solution)/shard_map/ppermute | solution.py:14
  71.2 4.3 %collective-permute-start.10 = (bf16[10,1,512]{2,1,0:T(2,128)(2,1)S(1)}, bf16[10,1,512]{2,1,0:T(2,128)(2,1)S(1)}, u32[]{:S(2)}, u32[]{:S(2)}) collective-permute-start(bf16[10,1,512]{2,1,0:T(2,128)(2,1)S(1)} %get-tuple-element.79), channel_id=1, source_target_pairs={{0,1},{1,2},{2,3},{4,5},{5,6},{6,7},{8,9},{9,10},{10,11},{12,13},{... | collective-permute-start | bytes 30728 | tf_op jit(solution)/shard_map/ppermute | solution.py:14
  72.5 7.8 %collective-permute-start.11 = (bf16[10,1,512]{2,1,0:T(2,128)(2,1)S(1)}, bf16[10,1,512]{2,1,0:T(2,128)(2,1)S(1)}, u32[]{:S(2)}, u32[]{:S(2)}) collective-permute-start(bf16[10,1,512]{2,1,0:T(2,128)(2,1)S(1)} %get-tuple-element.80), channel_id=1, source_target_pairs={{1,0},{2,1},{3,2},{5,4},{6,5},{7,6},{9,8},{10,9},{11,10},{13,12},{... | collective-permute-start | bytes 30728 | tf_op jit(solution)/shard_map/ppermute | solution.py:15
  81.5 27.2 %copy-start.17 = (bf16[8,16,512]{2,1,0:T(8,128)(2,1)S(1)}, bf16[8,16,512]{2,1,0:T(8,128)(2,1)}, u32[]{:S(2)}) copy-start(bf16[8,16,512]{2,1,0:T(8,128)(2,1)} %get-tuple-element.86) | copy-start | bytes 393220
  117.8 27.3 %slice-start = ((s8[4718592]{0:T(1024)(128)(4,1)}), s8[524288]{0:T(1024)(128)(4,1)S(1)}, s32[]{:S(2)}) async-start(s8[4718592]{0:T(1024)(128)(4,1)} %bitcast.323), calls=%async_computation.2 | async-start | bytes 1048576
  120.7 10.4 %collective-permute-start.13 = (bf16[1,16,512]{2,1,0:T(8,128)(2,1)}, bf16[1,16,512]{2,1,0:T(8,128)(2,1)}, u32[]{:S(2)}, u32[]{:S(2)}) collective-permute-start(bf16[1,16,512]{2,1,0:T(8,128)(2,1)} %get-tuple-element.84), channel_id=1, source_target_pairs={{4,0},{8,4},{12,8},{16,12},{20,16},{24,20},{28,24},{5,1},{9,5},{13... | collective-permute-start | bytes 49160 | tf_op jit(solution)/shard_map/ppermute | solution.py:15
  122.0 9.1 %collective-permute-start.12 = (bf16[1,16,512]{2,1,0:T(8,128)(2,1)}, bf16[1,16,512]{2,1,0:T(8,128)(2,1)}, u32[]{:S(2)}, u32[]{:S(2)}) collective-permute-start(bf16[1,16,512]{2,1,0:T(8,128)(2,1)} %get-tuple-element.83), channel_id=1, source_target_pairs={{0,4},{4,8},{8,12},{12,16},{16,20},{20,24},{24,28},{1,5},{5,9},{9,... | collective-permute-start | bytes 49160 | tf_op jit(solution)/shard_map/ppermute | solution.py:14
  129.0 16.1 %slice-start.1 = ((s8[4718592]{0:T(1024)(128)(4,1)}), s8[4194304]{0:T(1024)(128)(4,1)S(1)}, s32[]{:S(2)}) async-start(s8[4718592]{0:T(1024)(128)(4,1)} %bitcast.323), calls=%async_computation.3 | async-start | bytes 8388608
  131.9 8.2 %collective-permute-start.14 = (bf16[10,1,512]{2,1,0:T(2,128)(2,1)S(1)}, bf16[10,1,512]{2,1,0:T(2,128)(2,1)S(1)}, u32[]{:S(2)}, u32[]{:S(2)}) collective-permute-start(bf16[10,1,512]{2,1,0:T(2,128)(2,1)S(1)} %get-tuple-element.75), channel_id=1, source_target_pairs={{1,0},{2,1},{3,2},{5,4},{6,5},{7,6},{9,8},{10,9},{11,10},{13,12},{... | collective-permute-start | bytes 30728 | tf_op jit(solution)/shard_map/ppermute | solution.py:15
  133.2 6.9 %collective-permute-start.15 = (bf16[10,1,512]{2,1,0:T(2,128)(2,1)S(1)}, bf16[10,1,512]{2,1,0:T(2,128)(2,1)S(1)}, u32[]{:S(2)}, u32[]{:S(2)}) collective-permute-start(bf16[10,1,512]{2,1,0:T(2,128)(2,1)S(1)} %get-tuple-element.76), channel_id=1, source_target_pairs={{0,1},{1,2},{2,3},{4,5},{5,6},{6,7},{8,9},{9,10},{10,11},{12,13},{... | collective-permute-start | bytes 30728 | tf_op jit(solution)/shard_map/ppermute | solution.py:14
  152.4 8.1 %collective-permute-start.17 = (bf16[1,32,256]{2,1,0:T(8,128)(2,1)}, bf16[1,32,256]{2,1,0:T(8,128)(2,1)}, u32[]{:S(2)}, u32[]{:S(2)}) collective-permute-start(bf16[1,32,256]{2,1,0:T(8,128)(2,1)} %get-tuple-element.56), channel_id=1, source_target_pairs={{4,0},{8,4},{12,8},{16,12},{20,16},{24,20},{28,24},{5,1},{9,5},{13... | collective-permute-start | bytes 49160 | tf_op jit(solution)/shard_map/ppermute | solution.py:15
  153.7 6.8 %collective-permute-start.16 = (bf16[1,32,256]{2,1,0:T(8,128)(2,1)}, bf16[1,32,256]{2,1,0:T(8,128)(2,1)}, u32[]{:S(2)}, u32[]{:S(2)}) collective-permute-start(bf16[1,32,256]{2,1,0:T(8,128)(2,1)} %get-tuple-element.55), channel_id=1, source_target_pairs={{0,4},{4,8},{8,12},{12,16},{16,20},{20,24},{24,28},{1,5},{5,9},{9,... | collective-permute-start | bytes 49160 | tf_op jit(solution)/shard_map/ppermute | solution.py:14
  161.2 7.8 %collective-permute-start.18 = (bf16[18,1,256]{2,1,0:T(2,128)(2,1)S(1)}, bf16[18,1,256]{2,1,0:T(2,128)(2,1)S(1)}, u32[]{:S(2)}, u32[]{:S(2)}) collective-permute-start(bf16[18,1,256]{2,1,0:T(2,128)(2,1)S(1)} %get-tuple-element.47), channel_id=1, source_target_pairs={{1,0},{2,1},{3,2},{5,4},{6,5},{7,6},{9,8},{10,9},{11,10},{13,12},{... | collective-permute-start | bytes 27656 | tf_op jit(solution)/shard_map/ppermute | solution.py:15
  162.5 6.5 %collective-permute-start.19 = (bf16[18,1,256]{2,1,0:T(2,128)(2,1)S(1)}, bf16[18,1,256]{2,1,0:T(2,128)(2,1)S(1)}, u32[]{:S(2)}, u32[]{:S(2)}) collective-permute-start(bf16[18,1,256]{2,1,0:T(2,128)(2,1)S(1)} %get-tuple-element.48), channel_id=1, source_target_pairs={{0,1},{1,2},{2,3},{4,5},{5,6},{6,7},{8,9},{9,10},{10,11},{12,13},{... | collective-permute-start | bytes 27656 | tf_op jit(solution)/shard_map/ppermute | solution.py:14
  179.0 6.0 %collective-permute-start.21 = (bf16[1,64,128]{2,1,0:T(8,128)(2,1)S(1)}, bf16[1,64,128]{2,1,0:T(8,128)(2,1)S(1)}, u32[]{:S(2)}, u32[]{:S(2)}) collective-permute-start(bf16[1,64,128]{2,1,0:T(8,128)(2,1)S(1)} %get-tuple-element.28), channel_id=1, source_target_pairs={{4,0},{8,4},{12,8},{16,12},{20,16},{24,20},{28,24},{5,1},{9,5},{13... | collective-permute-start | bytes 49160 | tf_op jit(solution)/shard_map/ppermute | solution.py:15
  180.3 4.7 %collective-permute-start.20 = (bf16[1,64,128]{2,1,0:T(8,128)(2,1)S(1)}, bf16[1,64,128]{2,1,0:T(8,128)(2,1)S(1)}, u32[]{:S(2)}, u32[]{:S(2)}) collective-permute-start(bf16[1,64,128]{2,1,0:T(8,128)(2,1)S(1)} %get-tuple-element.27), channel_id=1, source_target_pairs={{0,4},{4,8},{8,12},{12,16},{16,20},{20,24},{24,28},{1,5},{5,9},{9,... | collective-permute-start | bytes 49160 | tf_op jit(solution)/shard_map/ppermute | solution.py:14
  185.0 6.5 %collective-permute-start.22 = (bf16[34,1,128]{2,1,0:T(2,128)(2,1)S(1)}, bf16[34,1,128]{2,1,0:T(2,128)(2,1)S(1)}, u32[]{:S(2)}, u32[]{:S(2)}) collective-permute-start(bf16[34,1,128]{2,1,0:T(2,128)(2,1)S(1)} %get-tuple-element.19), channel_id=1, source_target_pairs={{1,0},{2,1},{3,2},{5,4},{6,5},{7,6},{9,8},{10,9},{11,10},{13,12},{... | collective-permute-start | bytes 26120 | tf_op jit(solution)/shard_map/ppermute | solution.py:15
  186.3 6.0 %collective-permute-start.23 = (bf16[34,1,128]{2,1,0:T(2,128)(2,1)S(1)}, bf16[34,1,128]{2,1,0:T(2,128)(2,1)S(1)}, u32[]{:S(2)}, u32[]{:S(2)}) collective-permute-start(bf16[34,1,128]{2,1,0:T(2,128)(2,1)S(1)} %get-tuple-element.20), channel_id=1, source_target_pairs={{0,1},{1,2},{2,3},{4,5},{5,6},{6,7},{8,9},{9,10},{10,11},{12,13},{... | collective-permute-start | bytes 26120 | tf_op jit(solution)/shard_map/ppermute | solution.py:14
  195.6 119.9 %copy-start.1 = (bf16[512,256]{1,0:T(8,128)(2,1)S(1)}, bf16[512,256]{1,0:T(8,128)(2,1)}, u32[]{:S(2)}) copy-start(bf16[512,256]{1,0:T(8,128)(2,1)} %param.19) | copy-start | bytes 786436
  (28 other events, 126.6 us)
Sparse Core Ops, SparseCore 0:
  13.9 93.3 all-gather.1
  185.1 128.4 all-reduce.1
where the time goes:
time: 325 us; the launch traced here: 322 us
  waiting for transfers between devices  165 us (51%)
  starting transfers between devices  59.3 us (18%)
  matrix products  38 us (12%)
  other arithmetic  24.5 us (8%)
  local copies, waits for them, and re-layouts  20.1 us (6%)
  between operations  15.3 us (5%)
    psum x1, waiting for transfers between devices, shards(): sharpest_filter_derivative = lax.psum(local_grad, ('gy', 'gx')) * scale  117 us
    ppermute x12, starting transfers between devices, with_halo(): before = lax.ppermute(last, axis, up)  43.7 us
    all_gather x1, waiting for transfers between devices, shards(): lax.all_gather(coarse_kernel, 'gx', axis=3, tiled=True)  24.3 us
    ppermute x12, waiting for transfers between devices, with_halo(): after = lax.ppermute(leading, axis, down)  22.3 us
    dot_general x27, matrix products, conv_valid(): jnp.dot(window, kernel[row_off, col_off], preferred_element_type=jnp.floa...  17.2 us
    ppermute x12, starting transfers between devices, with_halo(): after = lax.ppermute(leading, axis, down)  15.5 us
    dot_general x27, matrix products, convt_valid(): lax.dot_general(window, kernel[row_off, col_off], (((1,), (1,)), ((), ())...  13.8 us
    concatenate x11, other arithmetic, with_halo(): x = jnp.concatenate([before, x, after], axis=dim)  8.09 us
  transfers between devices with their start and end apart: 26, of which 7 were waited for; matrix products, arithmetic and copies ran while one was open for 13% of the time, Pallas kernels for 0%

commit v1 on v0

--- a/solution.py
+++ b/solution.py
@@ -1,20 +1,327 @@
+import functools
+
 import jax
 import jax.numpy as jnp
 from jax import lax
+from jax.experimental import pallas as pl
+from jax.experimental.pallas import tpu as pltpu
 from jax.sharding import PartitionSpec as P
 
-
-def with_halo(x, sides, width):
-    for axis, dim in sides:
-        size, length = (lax.axis_size(axis), x.shape[dim])
-        up = [(i, (i + 1) % size) for i in range(size - 1)]
-        down = [(j, i) for i, j in up]
-        last = lax.slice_in_dim(x, length - width, length, axis=dim)
-        leading = lax.slice_in_dim(x, 0, width, axis=dim)
-        before = lax.ppermute(last, axis, up)
-        after = lax.ppermute(leading, axis, down)
-        x = jnp.concatenate([before, x, after], axis=dim)
-    return x
+MESH = pl.DeviceIdType.MESH
+ANY = pl.BlockSpec(memory_space=pl.ANY)
+VMEM = pl.BlockSpec(memory_space=pltpu.VMEM)
+
+DIRS = ((-1, 0), (1, 0), (0, -1), (0, 1), (-1, -1), (-1, 1), (1, -1), (1, 1))
+OPP = (1, 0, 3, 2, 7, 6, 5, 4)
+
+
+def halo_kernel(ny, nx, rows_in, cols_in, corn_in, rows_out, cols_out, corn_out, send, recv):
+    y, x = lax.axis_index("gy"), lax.axis_index("gx")
+
+    def exists(d):
+        dy, dx = DIRS[d]
+        ok = True
+        if dy < 0:
+            ok = y > 0
+        if dy > 0:
+            ok = y < ny - 1
+        if dx != 0:
+            okx = x > 0 if dx < 0 else x < nx - 1
+            ok = okx if dy == 0 else jnp.logical_and(ok, okx)
+        return ok
+
+    def part(d, rows, cols, corn):
+        return rows.at[d] if d < 2 else cols.at[d - 2] if d < 4 else corn.at[d - 4]
+
+    def copy(d):
+        return pltpu.make_async_remote_copy(
+            src_ref=part(d, rows_in, cols_in, corn_in),
+            dst_ref=part(OPP[d], rows_out, cols_out, corn_out),
+            send_sem=send.at[d],
+            recv_sem=recv.at[OPP[d]],
+            device_id=(y + DIRS[d][0], x + DIRS[d][1]),
+            device_id_type=MESH,
+        )
+
+    def landing(d):
+        return pltpu.make_async_remote_copy(
+            src_ref=part(d, rows_in, cols_in, corn_in),
+            dst_ref=part(d, rows_out, cols_out, corn_out),
+            send_sem=send.at[d],
+            recv_sem=recv.at[d],
+            device_id=(y + DIRS[d][0], x + DIRS[d][1]),
+            device_id_type=MESH,
+        )
+
+    barrier = pltpu.get_barrier_semaphore()
+    for d in range(8):
+
+        @pl.when(exists(d))
+        def _(d=d):
+            pl.semaphore_signal(
+                barrier, inc=1, device_id=(y + DIRS[d][0], x + DIRS[d][1]), device_id_type=MESH
+            )
+
+    above_below = jnp.minimum(y, 1) + jnp.minimum(ny - 1 - y, 1)
+    sideways = jnp.minimum(x, 1) + jnp.minimum(nx - 1 - x, 1)
+    pl.semaphore_wait(barrier, (above_below + 1) * (sideways + 1) - 1)
+
+    for d in range(8):
+
+        @pl.when(exists(d))
+        def _(d=d):
+            copy(d).start()
+
+    for d in range(8):
+
+        @pl.when(exists(d))
+        def _(d=d):
+            copy(d).wait_send()
+            landing(d).wait_recv()
+
+
+def with_halo(x, call_id):
+    h, w, c = x.shape
+    ny, nx = lax.axis_size("gy"), lax.axis_size("gx")
+    y, xx = lax.axis_index("gy"), lax.axis_index("gx")
+    rows = jnp.stack([x[0], x[h - 1]])
+    cols = jnp.stack([x[:, 0], x[:, w - 1]])
+    corners = jnp.stack([x[0, 0], x[0, w - 1], x[h - 1, 0], x[h - 1, w - 1]])
+    corners = jnp.broadcast_to(corners[:, None, :], (4, 16, c))
+    rows, cols, corners = pl.pallas_call(
+        functools.partial(halo_kernel, ny, nx),
+        out_shape=[jax.ShapeDtypeStruct(a.shape, a.dtype) for a in (rows, cols, corners)],
+        in_specs=[VMEM] * 3,
+        out_specs=[VMEM] * 3,
+        scratch_shapes=[pltpu.SemaphoreType.DMA((8,)), pltpu.SemaphoreType.DMA((8,))],
+        compiler_params=pltpu.CompilerParams(collective_id=call_id, has_side_effects=True),
+        name="halo",
+    )(rows, cols, corners)
+    zero = jnp.zeros((), x.dtype)
+    has_y = jnp.stack([y > 0, y < ny - 1])
+    has_x = jnp.stack([xx > 0, xx < nx - 1])
+    rows = jnp.where(has_y[:, None, None], rows, zero)
+    cols = jnp.where(has_x[:, None, None], cols, zero)
+    has = (has_y[:, None] & has_x[None, :]).reshape(4)
+    corners = jnp.where(has[:, None], corners[:, 0], zero)
+    top = jnp.concatenate([corners[0][None], rows[0], corners[1][None]], axis=0)
+    bottom = jnp.concatenate([corners[2][None], rows[1], corners[3][None]], axis=0)
+    middle = jnp.concatenate([cols[0][:, None], x, cols[1][:, None]], axis=1)
+    return jnp.concatenate([top[None], middle, bottom[None]], axis=0)
+
+
+def strip_kernel(ny, nx, body_in, edge_in, body_out, edge_out, send, recv):
+    y, x = lax.axis_index("gy"), lax.axis_index("gx")
+    links = [(0, k) for k in range(1, nx)]
+    links += [(dy, k) for dy in (-1, 1) for k in range(nx)]
+
+    def when(dy, run):
+        if dy == 0:
+            run()
+        else:
+            pl.when(y > 0 if dy < 0 else y < ny - 1)(run)
+
+    def copy(i, slot_of):
+        dy, k = links[i]
+        other = lax.rem(x + k, nx)
+        if dy == 0:
+            src, dst = body_in, body_out.at[slot_of(k)]
+        else:
+            src, dst = edge_in.at[0 if dy < 0 else 1], edge_out.at[1 if dy < 0 else 0, slot_of(k)]
+        return pltpu.make_async_remote_copy(
+            src_ref=src,
+            dst_ref=dst,
+            send_sem=send.at[i],
+            recv_sem=recv.at[i],
+            device_id=(y + dy, other),
+            device_id_type=MESH,
+        )
+
+    def landing(i):
+        dy, k = links[i]
+        source = lax.rem(x - k + nx, nx)
+        if dy == 0:
+            src, dst = body_in, body_out.at[source]
+        else:
+            src, dst = edge_in.at[0 if dy < 0 else 1], edge_out.at[1 if dy < 0 else 0, source]
+        return pltpu.make_async_remote_copy(
+            src_ref=src,
+            dst_ref=dst,
+            send_sem=send.at[i],
+            recv_sem=recv.at[i],
+            device_id=(y - dy, source),
+            device_id_type=MESH,
+        )
+
+    barrier = pltpu.get_barrier_semaphore()
+    for dy, k in links:
+
+        def greet(dy=dy, k=k):
+            pl.semaphore_signal(
+                barrier, inc=1, device_id=(y + dy, lax.rem(x + k, nx)), device_id_type=MESH
+            )
+
+        when(dy, greet)
+    above_below = jnp.minimum(y, 1) + jnp.minimum(ny - 1 - y, 1)
+    pl.semaphore_wait(barrier, nx - 1 + above_below * nx)
+    for i in range(len(links)):
+        when(links[i][0], lambda i=i: copy(i, lambda k: x).start())
+    for i in range(len(links)):
+        when(links[i][0], lambda i=i: copy(i, lambda k: x).wait_send())
+        when(-links[i][0], lambda i=i: landing(i).wait_recv())
+
+
+def gather_strip(block, reach, call_id):
+    h, w, c = block.shape
+    ny, nx = lax.axis_size("gy"), lax.axis_size("gx")
+    y, x = lax.axis_index("gy"), lax.axis_index("gx")
+    body = block.reshape(h * w, c)
+    edges = jnp.stack([block[:reach], block[h - reach :]]).reshape(2, reach * w, c)
+    count = nx - 1 + 2 * nx
+    got, rims = pl.pallas_call(
+        functools.partial(strip_kernel, ny, nx),
+        out_shape=[
+            jax.ShapeDtypeStruct((nx, h * w, c), block.dtype),
+            jax.ShapeDtypeStruct((2, nx, reach * w, c), block.dtype),
+        ],
+        in_specs=[VMEM] * 2,
+        out_specs=[VMEM] * 2,
+        scratch_shapes=[pltpu.SemaphoreType.DMA((count,)), pltpu.SemaphoreType.DMA((count,))],
+        compiler_params=pltpu.CompilerParams(collective_id=call_id, has_side_effects=True),
+        name="strip",
+    )(body, edges)
+    zero = jnp.zeros((), block.dtype)
+    mine = (jnp.arange(nx) == x)[:, None, None]
+    got = jnp.where(mine, body[None], got).reshape(nx, h, w, c)
+    has = jnp.stack([y > 0, y < ny - 1])[:, None, None, None]
+    rims = jnp.where(has, rims, zero).reshape(2, nx, reach, w, c)
+    full = jnp.concatenate([rims[0], got, rims[1]], axis=1)
+    return full.transpose(1, 0, 2, 3).reshape(h + 2 * reach, nx * w, c)
+
+
+def swap_kernel(nx, blocks, out, send, recv):
+    y, x = lax.axis_index("gy"), lax.axis_index("gx")
+
+    def copy(k, src_slot, dst_slot, device):
+        return pltpu.make_async_remote_copy(
+            src_ref=blocks.at[src_slot],
+            dst_ref=out.at[dst_slot],
+            send_sem=send.at[k],
+            recv_sem=recv.at[k],
+            device_id=(y, device),
+            device_id_type=MESH,
+        )
+
+    barrier = pltpu.get_barrier_semaphore()
+    for k in range(1, nx):
+        pl.semaphore_signal(
+            barrier, inc=1, device_id=(y, lax.rem(x + k, nx)), device_id_type=MESH
+        )
+    pl.semaphore_wait(barrier, nx - 1)
+    for k in range(1, nx):
+        to = lax.rem(x + k, nx)
+        copy(k, to, x, to).start()
+    for k in range(1, nx):
+        to = lax.rem(x + k, nx)
+        source = lax.rem(x - k + nx, nx)
+        copy(k, to, x, to).wait_send()
+        copy(k, to, source, source).wait_recv()
+
+
+def swap_blocks(blocks, call_id):
+    nx = lax.axis_size("gx")
+    got = pl.pallas_call(
+        functools.partial(swap_kernel, nx),
+        out_shape=jax.ShapeDtypeStruct(blocks.shape, blocks.dtype),
+        in_specs=[VMEM],
+        out_specs=VMEM,
+        scratch_shapes=[pltpu.SemaphoreType.DMA((nx,)), pltpu.SemaphoreType.DMA((nx,))],
+        compiler_params=pltpu.CompilerParams(collective_id=call_id, has_side_effects=True),
+        name="swap",
+    )(blocks)
+    mine = (jnp.arange(nx) == lax.axis_index("gx"))[:, None, None]
+    return jnp.where(mine, blocks, got)
+
+
+def sum_kernel(ny, nx, src, out, got_y, got_x, s1, r1, s2, r2, s3, r3):
+    y, x = lax.axis_index("gy"), lax.axis_index("gx")
+    f32 = jnp.float32
+
+    def copy(a, b, s, r, device):
+        return pltpu.make_async_remote_copy(
+            src_ref=a, dst_ref=b, send_sem=s, recv_sem=r, device_id=device, device_id_type=MESH
+        )
+
+    def over_y(k):
+        return (lax.rem(y + k, ny), x)
+
+    def over_x(k):
+        return (y, lax.rem(x + k, nx))
+
+    barrier = pltpu.get_barrier_semaphore()
+    for k in range(1, ny):
+        pl.semaphore_signal(barrier, inc=1, device_id=over_y(k), device_id_type=MESH)
+    for k in range(1, nx):
+        pl.semaphore_signal(barrier, inc=1, device_id=over_x(k), device_id_type=MESH)
+    pl.semaphore_wait(barrier, ny + nx - 2)
+
+    for k in range(1, ny):
+        to = over_y(k)
+        copy(src.at[to[0]], got_y.at[k], s1.at[k], r1.at[k], to).start()
+    total = src[y].astype(f32)
+    for k in range(1, ny):
+        to = over_y(k)
+        copy(src.at[to[0]], got_y.at[k], s1.at[k], r1.at[k], to).wait()
+        total = total + got_y[k].astype(f32)
+    got_x[x] = total.astype(got_x.dtype)
+
+    for k in range(1, nx):
+        copy(got_x.at[x], got_x.at[x], s2.at[k], r2.at[k], over_x(k)).start()
+    for k in range(1, nx):
+        source = lax.rem(x - k + nx, nx)
+        copy(got_x.at[x], got_x.at[x], s2.at[k], r2.at[k], over_x(k)).wait_send()
+        copy(got_x.at[x], got_x.at[source], s2.at[k], r2.at[k], over_x(k)).wait_recv()
+    total = got_x[0].astype(f32)
+    for p in range(1, nx):
+        total = total + got_x[p].astype(f32)
+    out[y] = total.astype(out.dtype)
+
+    for k in range(1, ny):
+        copy(out.at[y], out.at[y], s3.at[k], r3.at[k], over_y(k)).start()
+    for k in range(1, ny):
+        source = lax.rem(y - k + ny, ny)
+        copy(out.at[y], out.at[y], s3.at[k], r3.at[k], over_y(k)).wait_send()
+        copy(out.at[y], out.at[source], s3.at[k], r3.at[k], over_y(k)).wait_recv()
+
+
+def sum_all(term, call_id):
+    ny, nx = lax.axis_size("gy"), lax.axis_size("gx")
+    lanes = term.shape[-1]
+    flat = term.reshape(-1, lanes)
+    part = -(-flat.shape[0] // ny)
+    part = -(-part // 16) * 16
+    padded = jnp.pad(flat.astype(jnp.bfloat16), ((0, part * ny - flat.shape[0]), (0, 0)))
+    blocks = padded.reshape(ny, part, lanes)
+    dma = pltpu.SemaphoreType.DMA
+    total = pl.pallas_call(
+        functools.partial(sum_kernel, ny, nx),
+        out_shape=jax.ShapeDtypeStruct(blocks.shape, blocks.dtype),
+        in_specs=[VMEM],
+        out_specs=VMEM,
+        scratch_shapes=[
+            pltpu.VMEM((ny, part, lanes), jnp.bfloat16),
+            pltpu.VMEM((nx, part, lanes), jnp.bfloat16),
+            dma((ny,)),
+            dma((ny,)),
+            dma((nx,)),
+            dma((nx,)),
+            dma((ny,)),
+            dma((ny,)),
+        ],
+        compiler_params=pltpu.CompilerParams(collective_id=call_id, has_side_effects=True),
+        name="sum_all",
+    )(blocks)
+    return total.reshape(ny * part, lanes)[: flat.shape[0]].reshape(term.shape)
 
 
 def conv_valid(padded, kernel):
@@ -112,16 +419,10 @@
     return sig * (1.0 + value * (1.0 - sig))
 
 
-def rims_fine(field):
-    return with_halo(field, (("gy", 0), ("gx", 1)), 1)
-
-
-def rims_mid(field):
-    return with_halo(field, (("gy", 0), ("gx", 1)), 1)
-
-
-def rims_coarse(field):
-    return with_halo(field, (("gy", 0), ("gx", 1)), 1)
+def backward_start(cotangent, central_lifted_mixing):
+    back_mid = block_sum(cotangent).astype(jnp.bfloat16)
+    grad_mid = project_back(back_mid, central_lifted_mixing)
+    return grad_mid, block_sum(grad_mid).astype(jnp.bfloat16)
 
 
 def shards(
@@ -141,18 +442,37 @@
         features.astype(jnp.float32)
         + station_mask.astype(jnp.float32)[:, :, None] * station_gain[None, None, :]
     ).astype(jnp.bfloat16)
-    in_pad = rims_fine(inputs)
+    in_pad = with_halo(inputs, 0)
     pre_fine = conv_valid(in_pad, fine_kernel)
     sharpest_level_response = jax.nn.silu(pre_fine).astype(jnp.bfloat16)
     mid_in = pointwise_mixing_weights(pool_mean(sharpest_level_response), down_mid).astype(
         jnp.bfloat16
     )
-    pre_mid = conv_valid(rims_mid(mid_in), mid_kernel)
+    pre_mid = conv_valid(with_halo(mid_in, 1), mid_kernel)
     act_mid = jax.nn.silu(pre_mid).astype(jnp.bfloat16)
-    coarse_in = pointwise_mixing_weights(pool_mean(act_mid), down_coarse).astype(jnp.bfloat16)
-    coarse_pad = rims_coarse(coarse_in)
-    pre_coarse = conv_valid(coarse_pad, lax.all_gather(coarse_kernel, "gx", axis=3, tiled=True))
-    act_coarse = jax.nn.silu(pre_coarse).astype(jnp.bfloat16)
+    grad_mid, back_coarse = backward_start(cotangent, central_lifted_mixing)
+    x = lax.axis_index("gx")
+    nx = lax.axis_size("gx")
+    own_chans = coarse_kernel.shape[3]
+    own_up = lax.dynamic_slice_in_dim(up_coarse, x * own_chans, own_chans, axis=0)
+    pooled_mid = pool_mean(act_mid)
+    rows, cols, chans = pooled_mid.shape
+    strip = gather_strip(jnp.concatenate([pooled_mid, back_coarse], axis=2), 2, 2)
+    coarse_in = pointwise_mixing_weights(strip[:, :, :chans], down_coarse).astype(jnp.bfloat16)
+    pre_coarse = conv_valid(jnp.pad(coarse_in, ((0, 0), (1, 1), (0, 0))), coarse_kernel)
+    act_own = jax.nn.silu(pre_coarse[1 : 1 + rows]).astype(jnp.bfloat16)
+    delta_coarse = (
+        project_back(strip[1 : 3 + rows, :, chans:], own_up) * silu_slope(pre_coarse)
+    ).astype(jnp.bfloat16)
+    into_own = convt_valid(
+        jnp.pad(delta_coarse, ((0, 0), (1, 1), (0, 0))), coarse_kernel
+    ).astype(jnp.bfloat16)
+    down_own = project_back(into_own, down_coarse).astype(jnp.bfloat16)
+    blocks = jnp.concatenate([act_own, down_own], axis=2)
+    blocks = blocks.reshape(rows, nx, cols, -1).transpose(1, 0, 2, 3).reshape(nx, rows * cols, -1)
+    blocks = swap_blocks(blocks, 3)
+    act_coarse = blocks[:, :, :own_chans].transpose(1, 0, 2).reshape(rows, cols, nx * own_chans)
+    down_back = blocks[:, :, own_chans:].astype(jnp.float32).sum(axis=0).reshape(rows, cols, -1)
     ascend_central_level = (
         double_spatial_lattice(pointwise_mixing_weights(act_coarse, up_coarse))
         + act_mid.astype(jnp.float32)
@@ -163,20 +483,11 @@
         )
         + sharpest_level_response.astype(jnp.float32)
     ).astype(jnp.bfloat16)
-    back_mid = block_sum(cotangent).astype(jnp.bfloat16)
-    grad_mid = project_back(back_mid, central_lifted_mixing)
-    back_coarse = block_sum(grad_mid).astype(jnp.bfloat16)
-    delta_coarse = (project_back(back_coarse, up_coarse) * silu_slope(pre_coarse)).astype(
-        jnp.bfloat16
-    )
-    delta_pad = rims_coarse(delta_coarse)
-    into_total = convt_valid(delta_pad, lax.all_gather(coarse_kernel, "gx", axis=3, tiled=True))
-    into_coarse = into_total.astype(jnp.bfloat16)
     delta_mid = (
-        (grad_mid + double_spatial_lattice(project_back(into_coarse, down_coarse)) * 0.25)
+        (grad_mid + double_spatial_lattice(down_back) * 0.25)
         * silu_slope(pre_mid)
     ).astype(jnp.bfloat16)
-    into_mid = convt_valid(rims_mid(delta_mid), mid_kernel).astype(jnp.bfloat16)
+    into_mid = convt_valid(with_halo(delta_mid, 4), mid_kernel).astype(jnp.bfloat16)
     delta_fine = (
         (
             cotangent.astype(jnp.float32)
@@ -187,8 +498,8 @@
     local_grad = kernel_grad(in_pad, delta_fine)
     cells_all = features.shape[0] * lax.axis_size("gy") * features.shape[1] * lax.axis_size("gx")
     scale = 1.0 / jnp.sqrt(jnp.float32(cells_all))
-    sharpest_filter_derivative = lax.psum(local_grad, ("gy", "gx")) * scale
-    hidden_maps_sensitivity = convt_valid(rims_fine(delta_fine), fine_kernel).astype(jnp.bfloat16)
+    sharpest_filter_derivative = sum_all(local_grad, 6).astype(jnp.float32) * scale
+    hidden_maps_sensitivity = convt_valid(with_halo(delta_fine, 5), fine_kernel).astype(jnp.bfloat16)
     return (predicted_rainfall, hidden_maps_sensitivity, sharpest_filter_derivative)
 
 

time: 325 us -> 174 us (0.54)
  waiting for transfers between devices: 165 us -> 0 us
  Pallas kernels: 0 us -> 82.5 us
  starting transfers between devices: 59.3 us -> 0 us
  local copies, waits for them, and re-layouts: 20.1 us -> 36.4 us
  matrix products: 38 us -> 23 us
  between operations: 15.3 us -> 2.18 us
    psum x1 -> x0, waiting for transfers between devices: 117 us -> none  [shards(): sharpest_filter_derivative = lax.psum(local_grad, ('gy', 'gx')) * scale]
    pallas_call x0 -> x7, Pallas kernels: none -> 82.5 us  [the longest x4 28.7 us: with_halo(): pl.pallas_call(functools.partial(halo_kernel, ny, nx), out_shape=[jax.Sha...]
    ppermute x24 -> x0, starting transfers between devices: 59.2 us -> none  [the longest x12 43.7 us: with_halo(): before = lax.ppermute(last, axis, up)]
    all_gather x1 -> x0, waiting for transfers between devices: 24.3 us -> none  [shards(): lax.all_gather(coarse_kernel, 'gx', axis=3, tiled=True)]
    ppermute x24 -> x0, waiting for transfers between devices: 23.9 us -> none  [the longest x12 22.3 us: with_halo(): after = lax.ppermute(leading, axis, down)]
    dot_general x27, matrix products: 17.2 us -> 7.5 us  [conv_valid(): jnp.dot(window, kernel[row_off, col_off], preferred_element_type=jnp.floa...]
    select_n x0 -> x15, other arithmetic: none -> 9.23 us  [the longest x4 3.33 us: with_halo(): rows = jnp.where(has_y[:, None, None], rows, zero)]
    concatenate x11 -> x9, other arithmetic: 8.09 us -> 2.25 us  [the longest x4 1.38 us: with_halo(): return jnp.concatenate([top[None], middle, bottom[None]], axis=0)]
  transfers between devices with their start and end apart: 26 -> 0, of which waited for: 7 -> 0; matrix products, arithmetic and copies ran while one was open for 13% -> 0% of each run, Pallas kernels for 0% -> 0%
where the time goes in v1:
time: 174 us; the launch traced here: 172 us
  Pallas kernels  82.5 us (47%)
  local copies, waits for them, and re-layouts  36.4 us (21%)
  other arithmetic  27.6 us (16%)
  matrix products  23 us (13%)
  between operations  2.18 us (1%)
    pallas_call x4, Pallas kernels, with_halo(): pl.pallas_call(functools.partial(halo_kernel, ny, nx), out_shape=[jax.Sha...  28.7 us
    pallas_call x1, Pallas kernels, gather_strip(): pl.pallas_call(functools.partial(strip_kernel, ny, nx), out_shape=[jax.Sh...  21.6 us
    pallas_call x1, Pallas kernels, sum_all(): pl.pallas_call(functools.partial(sum_kernel, ny, nx), out_shape=jax.Shape...  19.7 us
    pallas_call x1, Pallas kernels, swap_blocks(): pl.pallas_call(functools.partial(swap_kernel, nx), out_shape=jax.ShapeDty...  12.5 us
    dot_general x27, matrix products, convt_valid(): lax.dot_general(window, kernel[row_off, col_off], (((1,), (1,)), ((), ())...  8.55 us
    dot_general x27, matrix products, conv_valid(): jnp.dot(window, kernel[row_off, col_off], preferred_element_type=jnp.floa...  7.5 us
    unnamed x40, local copies, waits for them, and re-layouts  7.15 us
    slice x21, local copies, waits for them, and re-layouts, conv_valid(): padded[row_off:row_off + rows, col_off:col_off + cols]  5.38 us

profile of v1, /device:TPU:0, one launch (start us, length us, event | category | flops | bytes accessed | tf_op | source)
XLA Modules:
  0.0 171.7 jit_solution(16656044621210408536)
XLA Ops:
  1.7 1.5 add_convert_fusion
  5.2 8.2 %halo.4 = (bf16[2,64,128]{2,1,0:T(8,128)(2,1)}, bf16[2,32,128]{2,1,0:T(8,128)(2,1)}, bf16[4,16,128]{2,1,0:T(8,128)(2,1)}) custom-call(bf16[2,64,128]{2,1,0:T(8,128)(2,1)} %copy.480.rows_in, bf16[2,32,128]{2,1,0:T(8,128)(2,1)} %pad_maximum_fusion.22.cols_in, bf16[4,16,128]{2,1,0:T(8,128)(2,1)} %broadcast_in_dim.231.corn_in), custom_call_target="tpu_custom_call" | custom-call | tf_op jit(solution)/shard_map/halo/pallas_call | solution.py:91
  15.0 0.8 broadcast_select_fusion.6
  16.5 0.9 reduce_sum.47
  27.4 5.9 %halo.5 = (bf16[2,32,256]{2,1,0:T(8,128)(2,1)}, bf16[2,16,256]{2,1,0:T(8,128)(2,1)}, bf16[4,16,256]{2,1,0:T(8,128)(2,1)}) custom-call(bf16[2,32,256]{2,1,0:T(8,128)(2,1)} %copy.496.rows_in, bf16[2,16,256]{2,1,0:T(8,128)(2,1)} %pad_maximum_fusion.23.cols_in, bf16[4,16,256]{2,1,0:T(8,128)(2,1)} %broadcast_in_dim.239.corn_in), custom_call_target="tpu_custom_call" | custom-call | tf_op jit(solution)/shard_map/halo/pallas_call | solution.py:91
  35.0 0.8 broadcast_select_fusion.4
  37.2 1.0 copy-done.7
  40.3 1.1 reshape.381
  41.4 1.2 convert_reduce_fusion.2
  43.9 21.6 %strip.1 = (bf16[4,128,512]{2,1,0:T(8,128)(2,1)}, bf16[2,4,32,512]{3,2,1,0:T(8,128)(2,1)}) custom-call(bf16[128,512]{1,0:T(8,128)(2,1)} %pad_maximum_fusion.14.body_in, bf16[2,32,512]{2,1,0:T(8,128)(2,1)} %pad_maximum_fusion.15.edge_in), custom_call_target="tpu_custom_call" | custom-call | tf_op jit(solution)/shard_map/strip/pallas_call | solution.py:181
  65.5 1.1 broadcast_select_fusion.2
  67.3 2.5 %pad_slice_fusion = (bf16[10,64,512]{2,1,0:T(8,128)(2,1)S(1)}, bf16[10,64,512]{2,1,0:T(8,128)(2,1)S(1)}, bf16[10,64,512]{2,1,0:T(8,128)(2,1)S(1)}, bf16[10,64,51...) fusion(bf16[12,64,512]{2,1,0:T(8,128)(2,1)S(1)} %convolution_co, ...), kind=kLoop, calls=%fused_computation.99 | loop fusion | bytes 8650752 | tf_op jit(solution)/shard_map/slice | solution.py:333
  72.8 1.1 fusion.3
  78.2 12.5 %swap.1 = bf16[4,128,384]{2,1,0:T(8,128)(2,1)} custom-call(bf16[4,128,384]{2,1,0:T(8,128)(2,1)} %bitcast.527), custom_call_target="tpu_custom_call" | custom-call | tf_op jit(solution)/shard_map/swap/pallas_call | solution.py:233
  90.8 1.2 broadcast_select_fusion.1
  92.2 1.1 fusion.35
  94.5 1.7 fusion.32
  96.2 0.9 copy.556
  99.1 9.0 %halo.6 = (bf16[2,32,256]{2,1,0:T(8,128)(2,1)}, bf16[2,16,256]{2,1,0:T(8,128)(2,1)}, bf16[4,16,256]{2,1,0:T(8,128)(2,1)}) custom-call(bf16[2,32,256]{2,1,0:T(8,128)(2,1)} %copy.523.rows_in, bf16[2,16,256]{2,1,0:T(8,128)(2,1)} %pad_maximum_fusion.24.cols_in, bf16[4,16,256]{2,1,0:T(8,128)(2,1)} %broadcast_in_dim.257.corn_in), custom_call_target="tpu_custom_call" | custom-call | tf_op jit(solution)/shard_map/halo/pallas_call | solution.py:91
  109.7 0.8 broadcast_select_fusion.3
  110.7 1.9 %broadcast_in_dim.256.clone = f32[16,16,2,256]{3,2,1,0:T(2,128)} broadcast(f32[16,16,256]{2,1,0:T(8,128)} %copy.556), dimensions={0,1,3} | broadcast | bytes 786432 | tf_op jit(solution)/shard_map/broadcast_in_dim | solution.py:396
  112.6 2.2 %mul.137 = f32[512,256]{1,0:T(8,128)} reshape(f32[16,16,2,256]{3,2,1,0:T(2,128)} %broadcast_in_dim.256.clone) | data formatting | bytes 1048576 | tf_op jit(solution)/shard_map/mul | solution.py:487
  114.8 1.0 broadcast_in_dim.252
  115.8 2.2 %reshape.407 = f32[512,256]{1,0:T(8,128)} reshape(f32[16,16,2,256]{3,2,1,0:T(2,128)} %broadcast_in_dim.252) | data formatting | bytes 1048576 | tf_op jit(solution)/shard_map/reshape | solution.py:396
  118.0 1.2 add_convert_fusion.1
  121.0 1.0 copy-done.8
  126.2 1.2 fusion.23
  127.3 1.0 copy.549
  134.2 19.7 %sum_all.1 = bf16[8,144,128]{2,1,0:T(8,128)(2,1)} custom-call(bf16[8,144,128]{2,1,0:T(8,128)(2,1)} %bitcast.562), custom_call_target="tpu_custom_call" | custom-call | tf_op jit(solution)/shard_map/sum_all/pallas_call | solution.py:306
  154.7 5.6 %halo.7 = (bf16[2,64,128]{2,1,0:T(8,128)(2,1)}, bf16[2,32,128]{2,1,0:T(8,128)(2,1)}, bf16[4,16,128]{2,1,0:T(8,128)(2,1)}) custom-call(bf16[2,64,128]{2,1,0:T(8,128)(2,1)} %copy.537.rows_in, bf16[2,32,128]{2,1,0:T(8,128)(2,1)} %pad_maximum_fusion.25.cols_in, bf16[4,16,128]{2,1,0:T(8,128)(2,1)} %broadcast_in_dim.262.corn_in), custom_call_target="tpu_custom_call" | custom-call | tf_op jit(solution)/shard_map/halo/pallas_call | solution.py:91
  162.9 1.8 %convert_multiply_fusion = f32[8,144,128]{2,1,0:T(8,128)} fusion(bf16[8,144,128]{2,1,0:T(8,128)(2,1)} %sum_all.1), kind=kLoop, calls=%fused_computation.105 | loop fusion | flops 294912 | bytes 884736 | tf_op jit(solution)/shard_map/mul | solution.py:501
  170.6 1.1 fusion
  (270 shorter events, 54.7 us)
Async XLA Ops:
  0.6 66.3 %copy-start = (bf16[256,512]{1,0:T(8,128)(2,1)S(1)}, bf16[256,512]{1,0:T(8,128)(2,1)}, u32[]{:S(2)}) copy-start(bf16[256,512]{1,0:T(8,128)(2,1)} %param.17) | copy-start | bytes 786436
  3.2 13.0 %copy-start.9 = (bf16[32,64,128]{2,1,0:T(8,128)(2,1)S(1)}, bf16[32,64,128]{2,1,0:T(8,128)(2,1)}, u32[]{:S(2)}) copy-start(bf16[32,64,128]{2,1,0:T(8,128)(2,1)} %param.21) | copy-start | bytes 1572868
  16.2 1.3 copy-start.17
  17.7 0.8 copy-start.4
  19.4 0.9 copy-start.2
  20.8 1.0 copy-start.11
  24.3 0.8 copy-start.16
  36.9 1.3 copy-start.7
  65.5 1.1 copy-start.15
  67.3 2.5 %copy-start.6 = (bf16[3,3,512,128]{3,2,1,0:T(8,128)(2,1)S(1)}, bf16[3,3,512,128]{3,2,1,0:T(8,128)(2,1)}, u32[]{:S(2)}) copy-start(bf16[3,3,512,128]{3,2,1,0:T(8,128)(2,1)} %param.18) | copy-start | bytes 3538948
  99.1 15.7 %copy-start.13 = (f32[8,2,16,256]{3,2,1,0:T(8,128)S(1)}, f32[8,2,16,256]{3,2,1,0:T(8,128)}, u32[]{:S(2)}) copy-start(f32[8,2,16,256]{3,2,1,0:T(8,128)} %broadcast_in_dim.251) | copy-start | bytes 786436
  115.8 3.4 %copy-start.18 = (bf16[256,128]{1,0:T(8,128)(2,1)S(1)}, bf16[256,128]{1,0:T(8,128)(2,1)}, u32[]{:S(2)}) copy-start(bf16[256,128]{1,0:T(8,128)(2,1)} %param.20) | copy-start | bytes 196612
  120.7 1.3 copy-start.8
  122.5 1.0 copy-start.5
  122.5 1.2 copy-start.14
  125.1 1.0 copy-start.10
  130.3 1.1 copy-start.3
  167.2 1.0 copy-start.12
  170.3 1.4 copy-start.1
